TPU v7x, 512 devices: a whole 4x4x16 slice. The times are simulated.
512 devices in a mesh: dp: 16 (over z), owner: 32 (over x, y, core).
Axes of the slice: x: 4, y: 4, z: 16, core: 2. Of those that a mesh axis runs over, the one named last changes fastest.
Arguments:
- grad_partials: bfloat16 [16, 32, 1048576], P('dp', None, 'owner'), may hold values from -2.5 to 2.5
- block_owner: int32 [32], replicated, may hold values from 0 to 31, as said below
- block_slot: int32 [32], replicated, may hold values from 0 to 1
- left_stat: float32 [64, 1024, 1024], P('owner', 'dp'), may hold values from -6 to 6
- right_stat: float32 [64, 1024, 1024], P('owner', 'dp'), may hold values from -6 to 6
- left_root: bfloat16 [64, 1024, 1024], P('owner', 'dp'), may hold values from -0.1875 to 0.1875
- right_root: bfloat16 [64, 1024, 1024], P('owner', 'dp'), may hold values from -0.1875 to 0.1875
Outputs:
- precond: bfloat16 [32, 1048576], P(None, ('dp', 'owner'))
- left_new: float32 [64, 1024, 1024], P('owner', 'dp')
- right_new: float32 [64, 1024, 1024], P('owner', 'dp')
Inputs may be any that keep to these rules, and one draw needn't show every extreme that they name: `block_owner`: blocks take distinct pairs of owner and slot; no owner holds more than 2 blocks, and some owner holds exactly 2.
All inputs are finite; a program needn't handle non-finite values.
Results may differ from a plain program's by a relative error of at most 0.025.
Values may be sent and summed in bfloat16 or wider, within the bound.
A program may use at most 64 MiB of HBM per device.

v0:
```python
import jax
import jax.numpy as jnp
from jax import lax
from jax.sharding import PartitionSpec as P

decay_rate = 0.95


def route_lookup(block_owner, block_slot, owners, capacity):
    target = block_slot * owners + block_owner
    places = jnp.arange(owners * capacity, dtype=jnp.int32)
    return (places[:, None] == target[None, :]).astype(jnp.bfloat16)


def shards(grad_partials, block_owner, block_slot, left_stat, right_stat, left_root, right_root):
    owners = lax.axis_size("owner")
    capacity = left_stat.shape[0]
    rows_here = left_stat.shape[1]
    block_width = left_stat.shape[2]
    lookup = route_lookup(block_owner, block_slot, owners, capacity)
    summands = grad_partials[0].astype(jnp.float32)
    summed = lax.psum(summands.astype(jnp.bfloat16), "dp")
    packed = jnp.dot(lookup, summed, preferred_element_type=jnp.float32).astype(jnp.bfloat16)
    packed = packed.reshape(capacity, owners, -1)
    arrived = lax.all_to_all(packed, "owner", split_axis=1, concat_axis=1, tiled=True)
    blocks = arrived.reshape(capacity, block_width, block_width)
    offset = lax.axis_index("dp") * rows_here
    own_rows = lax.dynamic_slice_in_dim(blocks, offset, rows_here, 1)
    own_columns = lax.dynamic_slice_in_dim(blocks, offset, rows_here, 2)
    left_gram = jnp.einsum("qrc,qsc->qrs", own_rows, blocks, preferred_element_type=jnp.float32)
    right_gram = jnp.einsum("qsr,qsc->qrc", own_columns, blocks, preferred_element_type=jnp.float32)
    left_new = decay_rate * left_stat + (1.0 - decay_rate) * left_gram
    right_new = decay_rate * right_stat + (1.0 - decay_rate) * right_gram
    scaled = jnp.einsum(
        "qrs,qsc->qrc", left_root, blocks, preferred_element_type=jnp.float32
    ).astype(jnp.bfloat16)
    combined = jnp.einsum(
        "qrk,qkc->qrc",
        scaled,
        lax.all_gather(right_root, "dp", axis=1, tiled=True),
        preferred_element_type=jnp.float32,
    )
    outgoing = combined.astype(jnp.bfloat16).reshape(capacity, owners, -1)
    returned = lax.all_to_all(outgoing, "owner", split_axis=1, concat_axis=1, tiled=True)
    stacked = returned.reshape(capacity * owners, -1)
    precond = jnp.dot(lookup.T, stacked, preferred_element_type=jnp.float32).astype(jnp.bfloat16)
    return (precond, left_new, right_new)


def solution(mesh):
    return jax.shard_map(
        shards,
        mesh=mesh,
        in_specs=(
            P("dp", None, "owner"),
            P(),
            P(),
            P("owner", "dp", None),
            P("owner", "dp", None),
            P("owner", "dp", None),
            P("owner", "dp", None),
        ),
        out_specs=(P(None, ("dp", "owner")), P("owner", "dp", None), P("owner", "dp", None)),
        check_vma=False,
    )
```

profile of v0, /device:TPU:1, one launch (start us, length us, event | category | flops | bytes accessed | tf_op | source)
XLA Modules:
  0.0 277.2 jit_solution(17667677478405312203)
XLA Ops:
  7.2 0.0 copy-start
  7.2 0.0 all-reduce.2.cloned.1.call-start
  7.2 0.7 all-reduce.2.cloned.1.call-update
  7.9 0.0 all-gather.2.cloned.1.call-start
  8.0 0.7 all-gather.2.cloned.1.call-update
  8.7 0.7 multiply_add_fusion
  9.3 141.7 %all-reduce.2.cloned.1.call-done = bf16[32,32768]{1,0:T(8,128)(2,1)} async-done(((bf16[32,32768]{1,0:T(8,128)(2,1)}), bf16[32,32768]{1,0:T(8,128)(2,1)}) %all-reduce.2.cloned.1.call-update) | async-done | bytes 2097168 | tf_op jit(solution)/shard_map/psum | solution.py:22
  151.0 2.8 %convolution_convert_fusion = bf16[64,32768]{1,0:T(8,128)(2,1)S(1)} fusion(bf16[32,32768]{1,0:T(8,128)(2,1)} %all-reduce.2.cloned.1.call-done, s32[32]{0:T(128)S(1)} %multiply_add_fusion), kind=kOutput, calls=%fused_computation | convolution fusion | flops 136316928 | bytes 6291584 | tf_op jit(solution)/shard_map/dot_general | solution.py:23
  153.9 6.3 %copy.15 = bf16[2,32,32768]{2,0,1:T(2,128)(2,1)} copy(bf16[2,32,32768]{2,1,0:T(8,128)(2,1)S(1)} %bitcast.10) | data formatting | bytes 8388608 | tf_op jit(solution)/shard_map/reshape | solution.py:24
  160.1 16.4 %all-to-all-start = ((bf16[2,32,32768]{2,0,1:T(2,128)(2,1)}), bf16[2,32,32768]{2,0,1:T(2,128)(2,1)}, u32[]{:S(2)}, u32[]{:S(2)}) async-start(bf16[2,32,32768]{2,0,1:T(2,128)(2,1)} %copy.15), calls=%async_computation | async-start | bytes 8388608 | tf_op jit(solution)/shard_map/all_to_all | solution.py:25
  176.6 52.2 %all-to-all-done = bf16[2,32,32768]{2,0,1:T(2,128)(2,1)} async-done(((bf16[2,32,32768]{2,0,1:T(2,128)(2,1)}), bf16[2,32,32768]{2,0,1:T(2,128)(2,1)}, u32[]{:S(2)}, u32[]{:S(2)}) %all-to-all-start) | async-done | bytes 4194336 | tf_op jit(solution)/shard_map/all_to_all | solution.py:25
  228.8 6.5 %copy.16 = bf16[2,32,32768]{2,1,0:T(8,128)(2,1)} copy(bf16[2,32,32768]{2,0,1:T(2,128)(2,1)} %all-to-all-done) | data formatting | bytes 8388608 | tf_op jit(solution)/shard_map/all_to_all | solution.py:25
  235.3 0.0 copy-start.1
  235.3 7.5 %reshape.20 = bf16[2,1024,1024]{2,1,0:T(8,128)(2,1)} reshape(bf16[2,32,32768]{2,1,0:T(8,128)(2,1)} %copy.16) | data formatting | bytes 8388608 | tf_op jit(solution)/shard_map/reshape | solution.py:26
  242.8 0.0 copy-done.1
  242.8 4.3 %fusion = f32[2,64,1024]{2,1,0:T(8,128)} fusion(bf16[2,1024,1024]{2,1,0:T(8,128)(2,1)} %reshape.20, s32[]{:T(128)S(6)} %select_n.4, f32[2,64,1024]{2,1,0:T(8,128)S(1)} %copy-done.1), kind=kOutput, calls=%fused_computation.3 | convolution fusion | flops 268828672 | bytes 5767172 | tf_op jit(solution)/shard_map/qsr,qsc->qrc/dot_general | solution.py:31
  247.1 0.0 copy-start.2
  247.1 0.0 all-gather.2.cloned.1.call-done
  247.1 0.0 copy-done
  247.1 5.1 %convolution_convert_fusion.3 = bf16[2,64,1024]{2,1,0:T(8,128)(2,1)S(1)} fusion(bf16[2,1024,1024]{2,1,0:T(8,128)(2,1)} %all-gather.2.cloned.1.call-done, bf16[2,64,1024]{2,1,0:T(8,128)(2,1)S(1)} %copy-done, bf16[2,1024,1024]{2,1,0:T(8,128)(2,1)} %reshape.20), kind=kOutput, calls=%fused_computation.7 | convolution fusion | flops 537133056 | bytes 8912896 | tf_op jit(solution)/shard_map/qrk,qkc->qrc/dot_general | solution.py:37
  252.2 0.1 reshape.21
  252.3 1.0 copy.17
  253.3 7.1 %all-to-all-start.1 = ((bf16[2,32,2048]{2,0,1:T(2,128)(2,1)}), bf16[2,32,2048]{2,0,1:T(2,128)(2,1)S(1)}, u32[]{:S(2)}, u32[]{:S(2)}) async-start(bf16[2,32,2048]{2,0,1:T(2,128)(2,1)} %copy.17), calls=%async_computation.1 | async-start | bytes 524288 | tf_op jit(solution)/shard_map/all_to_all | solution.py:44
  260.4 0.0 copy-done.2
  260.4 4.5 %fusion.1 = f32[2,64,1024]{2,1,0:T(8,128)} fusion(bf16[2,1024,1024]{2,1,0:T(8,128)(2,1)} %reshape.20, f32[2,64,1024]{2,1,0:T(8,128)S(1)} %copy-done.2, s32[]{:T(128)S(6)} %select_n.4), kind=kOutput, calls=%fused_computation.5 | convolution fusion | flops 268828672 | bytes 5505028 | tf_op jit(solution)/shard_map/qrc,qsc->qrs/dot_general | solution.py:30
  264.9 4.5 %all-to-all-done.1 = bf16[2,32,2048]{2,0,1:T(2,128)(2,1)S(1)} async-done(((bf16[2,32,2048]{2,0,1:T(2,128)(2,1)}), bf16[2,32,2048]{2,0,1:T(2,128)(2,1)S(1)}, u32[]{:S(2)}, u32[]{:S(2)}) %all-to-all-start.1) | async-done | bytes 262176 | tf_op jit(solution)/shard_map/all_to_all | solution.py:44
  269.4 0.1 copy.18
  269.5 0.9 convolution_convert_fusion.1
Async XLA Ops:
  7.2 239.9 %copy-start = (bf16[2,64,1024]{2,1,0:T(8,128)(2,1)S(1)}, bf16[2,64,1024]{2,1,0:T(8,128)(2,1)}, u32[]{:S(2)}) copy-start(bf16[2,64,1024]{2,1,0:T(8,128)(2,1)} %param.12) | copy-start | bytes 786436
  7.2 143.9 %all-reduce.2.cloned.1.call-start = ((), (), s32[]{:S(2)}) async-start(), calls=%async_computation.2 | async-start | bytes 4194304 | tf_op jit(solution)/shard_map/psum | solution.py:22
  7.9 239.2 %all-gather.2.cloned.1.call-start = ((), (), s32[]{:S(2)}) async-start(), calls=%async_computation.3 | async-start | bytes 4456448 | tf_op jit(solution)/shard_map/all_gather | solution.py:40
  160.1 68.7 %all-to-all-start = ((bf16[2,32,32768]{2,0,1:T(2,128)(2,1)}), bf16[2,32,32768]{2,0,1:T(2,128)(2,1)}, u32[]{:S(2)}, u32[]{:S(2)}) async-start(bf16[2,32,32768]{2,0,1:T(2,128)(2,1)} %copy.15), calls=%async_computation | async-start | bytes 8388608 | tf_op jit(solution)/shard_map/all_to_all | solution.py:25
  235.3 7.5 %copy-start.1 = (f32[2,64,1024]{2,1,0:T(8,128)S(1)}, f32[2,64,1024]{2,1,0:T(8,128)}, u32[]{:S(2)}) copy-start(f32[2,64,1024]{2,1,0:T(8,128)} %param.11) | copy-start | bytes 1572868
  247.1 13.3 %copy-start.2 = (f32[2,64,1024]{2,1,0:T(8,128)S(1)}, f32[2,64,1024]{2,1,0:T(8,128)}, u32[]{:S(2)}) copy-start(f32[2,64,1024]{2,1,0:T(8,128)} %param.10) | copy-start | bytes 1572868
  253.3 16.1 %all-to-all-start.1 = ((bf16[2,32,2048]{2,0,1:T(2,128)(2,1)}), bf16[2,32,2048]{2,0,1:T(2,128)(2,1)S(1)}, u32[]{:S(2)}, u32[]{:S(2)}) async-start(bf16[2,32,2048]{2,0,1:T(2,128)(2,1)} %copy.17), calls=%async_computation.1 | async-start | bytes 524288 | tf_op jit(solution)/shard_map/all_to_all | solution.py:44
Sparse Core Ops, SparseCore 0:
  10.4 140.6 all-reduce.1
  153.1 75.5 all-gather.1
where the time goes:
time: 278 us; the launch traced here: 277 us
  waiting for transfers between devices  200 us (72%)
  starting transfers between devices  23.6 us (8%)
  local copies, waits for them, and re-layouts  21.4 us (8%)
  matrix products  17.6 us (6%)
  between operations  14.1 us (5%)
    psum x1, waiting for transfers between devices, shards(): summed = lax.psum(summands.astype(jnp.bfloat16), 'dp')  142 us
    all_to_all x1, waiting for transfers between devices, shards(): lax.all_to_all(packed, 'owner', split_axis=1, concat_axis=1, tiled=True)  52.2 us
    all_to_all x1, starting transfers between devices, shards(): lax.all_to_all(packed, 'owner', split_axis=1, concat_axis=1, tiled=True)  16.4 us
    reshape x1, local copies, waits for them, and re-layouts, shards(): blocks = arrived.reshape(capacity, block_width, block_width)  7.53 us
    all_to_all x1, starting transfers between devices, shards(): lax.all_to_all(outgoing, 'owner', split_axis=1, concat_axis=1, tiled=True)  7.14 us
    all_to_all x1, local copies, waits for them, and re-layouts, shards(): lax.all_to_all(packed, 'owner', split_axis=1, concat_axis=1, tiled=True)  6.46 us
    reshape x1, local copies, waits for them, and re-layouts, shards(): packed = packed.reshape(capacity, owners, -1)  6.28 us
  transfers between devices with their start and end apart: 4, of which 3 were waited for; matrix products, arithmetic and copies ran while one was open for 12% of the time, Pallas kernels for 0%

commit v1 on v0

v1 whole, which is shorter than its diff:
```python
import functools

import jax
import jax.numpy as jnp
from jax import lax
from jax.experimental import pallas as pl
from jax.experimental.pallas import tpu as pltpu
from jax.sharding import PartitionSpec as P

decay_rate = 0.95

MESH = pl.DeviceIdType.MESH
BF16 = jnp.bfloat16
F32 = jnp.float32
PLANES = 16
OWNERS = 32
BLOCKS = 32
WIDTH = 1024
SUBS = 2


def iotas(rows, columns):
    return (
        lax.broadcasted_iota(jnp.int32, (rows, columns), 0),
        lax.broadcasted_iota(jnp.int32, (rows, columns), 1),
    )


def one_hot(hit):
    return jnp.where(hit, 1.0, 0.0).astype(BF16)


def mix(chooser, data):
    return jnp.dot(chooser, data, preferred_element_type=F32).astype(BF16)


def times_transposed(a, b):
    return lax.dot_general(a, b, (((1,), (1,)), ((), ())), preferred_element_type=F32)


def chunk(start, size, unit=None):
    return pl.ds(pl.multiple_of(start, unit or size), size)


def shuffles():
    m, k = iotas(256, 256)
    transpose16 = (m % 16) * 16 + m // 16
    roots_out = (((m >> 4) & 1) * 32 + ((m >> 3) & 1) * 16 + (m & 3) * 4) * 4 + (m >> 5) * 2 + ((m >> 2) & 1)
    stats_in = ((m >> 1) & 7) * 32 + (m >> 7) * 16 + ((m >> 6) & 1) * 8 + (m & 1) * 4 + ((m >> 4) & 3)
    roots_in = ((m >> 1) & 15) * 16 + (m >> 7) * 8 + (m & 1) * 4 + ((m >> 5) & 3)
    grams_out = ((((m >> 3) & 1) * 4 + (m & 3)) * 16 + (m >> 4)) * 2 + ((m >> 2) & 1)
    scaled_out = ((m & 7) * 16 + (m >> 4)) * 2 + ((m >> 3) & 1)
    right_rows = ((m >> 2) & 3) * 64 + (m >> 4) * 4 + (m & 3)
    return [one_hot(k == s) for s in (transpose16, roots_out, stats_in, roots_in, grams_out, scaled_out, right_rows)]


T16, ROOTS_OUT, STATS_IN, ROOTS_IN, GRAMS_OUT, SCALED_OUT, RIGHT_ROWS = range(7)


class Spread:
    def __init__(self, buf, send_sem, recv_sem, place):
        self.buf, self.send_sem, self.recv_sem = buf, send_sem, recv_sem
        self.z, self.x, self.y, self.c = place

    def chip(self, h, da, db):
        first, second = (self.x, self.y) if h == 0 else (self.y, self.x)
        first, second = (first + da) % 4, (second + db) % 4
        return (first, second) if h == 0 else (second, first)

    def piece(self, h, da, db, half=None):
        px, py = self.chip(h, da, db)
        start = px * 256 + py * 64 + (self.c if h == 0 else 1 - self.c) * 32
        if half is None:
            return self.buf.at[chunk(start, 32)]
        return self.buf.at[chunk(start + 16 * half, 16)]

    def copy(self, h, da, db, half, axis, delta):
        px, py = self.chip(h, delta if axis == 0 else 0, delta if axis == 1 else 0)
        there = ((da - delta) % 4, db) if axis == 0 else (da, (db - delta) % 4)
        ref = self.piece(h, da, db, half)
        return pltpu.make_async_remote_copy(
            src_ref=ref,
            dst_ref=ref,
            send_sem=self.send_sem,
            recv_sem=self.recv_sem.at[h, there[0], there[1], half or 0],
            device_id=(self.z, (px * 4 + py) * 2 + self.c),
            device_id_type=MESH,
        )

    def wait(self, h, da, db, half=None):
        ref = self.piece(h, da, db, half)
        pltpu.make_async_copy(ref, ref, self.recv_sem.at[h, da, db, half or 0]).wait()

    def across(self, h, da):
        for delta in (1, -1):
            self.copy(h, da, 0, None, 1, delta).start()

    def begin(self, h):
        for delta in (1, -1):
            self.copy(h, 0, 0, None, 0, delta).start()
        self.across(h, 0)

    def middle(self):
        for da, half, delta in ((3, 0, 1), (1, 1, -1)):
            for h in (0, 1):
                self.wait(h, da, 0)
                self.copy(h, da, 0, half, 0, delta).start()
                self.across(h, da)
        self.turn(0)
        for h in (0, 1):
            self.wait(h, 2, 0, 0)
            self.wait(h, 2, 0, 1)
            self.across(h, 2)
        self.turn(3)
        self.turn(1)
        self.turn(2)

    def turn(self, da):
        for db, half, delta in ((3, 0, 1), (1, 1, -1)):
            for h in (0, 1):
                self.wait(h, da, db)
                self.copy(h, da, db, half, 1, delta).start()

    def end(self):
        for da in (0, 3, 1, 2):
            for h in (0, 1):
                self.wait(h, da, 2, 0)
                self.wait(h, da, 2, 1)

    def sent(self):
        ref = self.buf.at[pl.ds(0, 960)]
        pltpu.make_async_copy(ref, ref, self.send_sem).wait()


class Column:
    def __init__(self, src, dst, sems, place):
        self.src, self.dst, self.sems = src, dst, sems
        self.z, self.chip, self.c = place

    def copy(self, zd, e):
        return pltpu.make_async_remote_copy(
            src_ref=self.src.at[chunk((2 * zd + e) * 16, 16)],
            dst_ref=self.dst.at[chunk((2 * self.z + self.c) * 16, 16)],
            send_sem=self.sems.at[0],
            recv_sem=self.sems.at[1],
            device_id=(zd, 2 * self.chip + e),
            device_id_type=MESH,
        )

    def start(self):
        def step(j, carry):
            for zd in ((self.z + j) % PLANES, (self.z + PLANES - j) % PLANES):
                for e in (0, 1):
                    self.copy(zd, e).start()
            return carry

        lax.fori_loop(1, PLANES // 2, step, 0)
        for e in (0, 1):
            self.copy((self.z + PLANES // 2) % PLANES, e).start()
        self.copy(self.z, 1 - self.c).start()
        own = chunk((2 * self.z + self.c) * 16, 16)
        self.dst[own, :] = self.src[own, :]

    def wait(self, which):
        ref = self.dst.at[pl.ds(0, 31 * 16)]
        pltpu.make_async_copy(ref, ref, self.sems.at[which]).wait()


class Plane:
    def __init__(self, src, dst, sems, place):
        self.src, self.dst, self.sems = src, dst, sems
        self.z, self.o = place

    def start(self):
        def step(j, carry):
            there = (self.o + j) % OWNERS
            pltpu.make_async_remote_copy(
                src_ref=self.src.at[chunk(there * 32, 32)],
                dst_ref=self.dst.at[chunk(self.o * 32, 32)],
                send_sem=self.sems.at[0],
                recv_sem=self.sems.at[1],
                device_id=(self.z, there),
                device_id_type=MESH,
            ).start()
            return carry

        lax.fori_loop(1, OWNERS, step, 0)
        own = chunk(self.o * 32, 32)
        self.dst[own, :] = self.src[own, :]

    def wait(self, which):
        ref = self.dst.at[pl.ds(0, 31 * 32)]
        pltpu.make_async_copy(ref, ref, self.sems.at[which]).wait()


def kernel(
    owner_ref, slot_ref, g_hbm, lstat_hbm, rstat_hbm, lroot_hbm, rroot_hbm,
    precond_ref, left_ref, right_ref,
    g, lstat, rstat, lroot, rroot, perm, parts, from_left, from_right, swapped, block,
    roots_out, roots_in, blocks_out, blocks_in, lsel, rheld, rfull,
    grams, zout, zin, stats_out, stats_in, pout, pin, to_blocks, to_places,
    load_sem, rs_send, right_sem, left_sem, swap_sem, block_send, block_recv, rheld_send, rheld_recv,
    a1_sem, a2_sem, zg_sem, zp_sem, f_sem,
):
    z, o = lax.axis_index("dp"), lax.axis_index("owner")
    chip, c = o // 2, o % 2
    x, y = chip // 4, chip % 4

    loads = [
        pltpu.make_async_copy(src, dst, load_sem.at[n])
        for n, (src, dst) in enumerate(
            ((g_hbm.at[0], g), (lroot_hbm, lroot), (rroot_hbm, rroot), (lstat_hbm, lstat), (rstat_hbm, rstat))
        )
    ]
    for load in loads:
        load.start()

    barrier = pltpu.get_barrier_semaphore()

    def greet_plane(j, carry):
        pl.semaphore_signal(barrier, inc=1, device_id=(z, (o + j) % OWNERS), device_id_type=MESH)
        return carry

    def greet_column(j, carry):
        for e in (0, 1):
            pl.semaphore_signal(barrier, inc=1, device_id=((z + j) % PLANES, 2 * chip + e), device_id_type=MESH)
        return carry

    lax.fori_loop(1, PLANES, greet_column, 0)
    lax.fori_loop(1, OWNERS, greet_plane, 0)

    for n, shuffle in enumerate(shuffles()):
        perm[n] = shuffle

    loads[0].wait()
    for h in range(2):
        for q in range(2):
            for w in range(4):
                columns = [(16 * q + r) * WIDTH + 256 * w for r in range(16)]
                stacked = jnp.concatenate([g[16 * h : 16 * h + 16, n : n + 256] for n in columns], axis=0)
                turned = mix(perm[T16], stacked)
                for b in range(16):
                    at = (b % 2) * 32 + 16 * q
                    parts[8 * h + b // 2, at : at + 16, 256 * w : 256 * w + 256] = turned[16 * b : 16 * b + 16]

    pl.semaphore_wait(barrier, OWNERS - 1 + 2 * (PLANES - 1))

    step_rows = 64 // SUBS

    def rs_copy(right, s, sub):
        rows = pl.ds(sub * step_rows, step_rows)
        held = from_left if right else from_right
        part = (z + 8 - s) % PLANES if right else (z + 9 + s) % PLANES
        sems = right_sem if right else left_sem
        return pltpu.make_async_remote_copy(
            src_ref=parts.at[part, rows] if s == 0 else held.at[s - 1, rows],
            dst_ref=held.at[s, rows],
            send_sem=rs_send,
            recv_sem=sems.at[s, sub],
            device_id=((z + (1 if right else PLANES - 1)) % PLANES, o),
            device_id_type=MESH,
        )

    def rs_step(right, s, sub):
        if s > 0:
            rs_copy(right, s - 1, sub).wait_recv()
            rows = pl.ds(sub * step_rows, step_rows)
            held = from_left if right else from_right
            part = (z + 8 - s) % PLANES if right else (z + 9 + s) % PLANES
            total = held[s - 1, rows, :].astype(F32) + parts[part, rows, :].astype(F32)
            held[s - 1, rows, :] = total.astype(BF16)
        rs_copy(right, s, sub).start()

    for sub in range(SUBS):
        rs_step(True, 0, sub)
        rs_step(False, 0, sub)

    loads[1].wait()
    loads[2].wait()
    for k in range(4):
        stacked = jnp.concatenate(
            [
                root[p, 16 * k : 16 * k + 16, 256 * q : 256 * q + 256]
                for p in range(2)
                for root in (lroot, rroot)
                for q in range(4)
            ],
            axis=0,
        )
        roots_out[256 * k : 256 * k + 256, :] = mix(perm[ROOTS_OUT], stacked)
    a1 = Plane(roots_out, roots_in, a1_sem, (z, o))
    a1.start()

    for sub in range(SUBS):
        rs_step(True, 1, sub)
        rs_step(False, 1, sub)

    places = [owner_ref[b] * 2 + slot_ref[b] for b in range(BLOCKS)]
    row, column = iotas(16, WIDTH)
    for b in range(BLOCKS):
        to_blocks[16 * b : 16 * b + 16, :] = one_hot(column == places[b] * 16 + row)
    column = lax.broadcasted_iota(jnp.int32, (1, 512), 1)
    target = jnp.zeros((1, 512), jnp.int32)
    for b in range(BLOCKS):
        target = jnp.where(column // 16 == b, places[b] * 16, target)
    target = target + column % 16
    for k in range(4):
        row = lax.broadcasted_iota(jnp.int32, (256, 512), 0) + 256 * k
        to_places[256 * k : 256 * k + 256, :] = one_hot(row == target)

    for s in (2, 3):
        for sub in range(SUBS):
            rs_step(True, s, sub)
            rs_step(False, s, sub)

    a1.wait(1)
    blocks_out[...] = mix(to_blocks[...], roots_in[...])

    for s in (4, 5, 6):
        for sub in range(SUBS):
            rs_step(True, s, sub)
            rs_step(False, s, sub)
    for sub in range(SUBS):
        rs_step(True, 7, sub)

    a2 = Column(blocks_out, blocks_in, a2_sem, (z, chip, c))
    a2.start()

    def last_sum(which):
        rows = chunk(which * 32, 32)
        for held, sems, s in ((from_left, right_sem, 7), (from_right, left_sem, 6)):
            if SUBS == 2:
                ref = held.at[s, rows]
                pltpu.make_async_copy(ref, ref, sems.at[s, which]).wait()
            else:
                for n in range(SUBS // 2):
                    ref = held.at[s, chunk(which * 32 + n * step_rows, step_rows)]
                    pltpu.make_async_copy(ref, ref, sems.at[s, which * (SUBS // 2) + n]).wait()
        total = parts[z, rows, :].astype(F32) + from_left[7, rows, :].astype(F32) + from_right[6, rows, :].astype(F32)
        return total.astype(BF16)

    def swap_copy(rows_of):
        return pltpu.make_async_remote_copy(
            src_ref=swapped,
            dst_ref=block.at[chunk(rows_of * 32, 32)],
            send_sem=swap_sem.at[0],
            recv_sem=swap_sem.at[1],
            device_id=(z, 2 * chip + 1 - c),
            device_id_type=MESH,
        )

    swapped[...] = last_sum(1 - c)
    swap_copy(o).start()
    block[chunk(o * 32, 32), :] = last_sum(c)
    spread = Spread(block, block_send, block_recv, (z, x, y, c))
    spread.begin(0)
    swap_copy(2 * chip + 1 - c).wait_recv()
    spread.begin(1)
    spread.middle()

    a2.wait(1)
    for h in range(2):
        turned = mix(perm[ROOTS_IN], blocks_in[256 * h : 256 * h + 256, :])
        for q in range(4):
            lsel[32 * h : 32 * h + 32, 256 * q : 256 * q + 256] = turned[32 * q : 32 * q + 32]
            rheld[chunk(chip * 64 + 32 * h, 32), 256 * q : 256 * q + 256] = turned[128 + 32 * q : 160 + 32 * q]
    rspread = Spread(rheld, rheld_send, rheld_recv, (z, x, y, c))
    rspread.begin(0)
    rspread.begin(1)

    spread.end()

    m, k = iotas(64, 256)
    chosen = one_hot(k == (m >> 2) * 16 + 4 * y + (m & 3))
    stacked = jnp.concatenate([block[chunk(64 * zz + 16 * x, 16), :] for zz in range(PLANES)], axis=0)
    lhs = mix(chosen, stacked)
    for q in range(4):
        grams[0, :, 256 * q : 256 * q + 256] = times_transposed(lhs, block[256 * q : 256 * q + 256, :]).astype(BF16)
    m, k = iotas(64, WIDTH)
    chosen = one_hot(k == (m >> 2) * 64 + 4 * chip + (m & 3))
    lhs = jnp.concatenate(
        [times_transposed(chosen, block[256 * q : 256 * q + 256, :]).astype(BF16) for q in range(4)], axis=1
    )
    for q in range(4):
        grams[1, :, 256 * q : 256 * q + 256] = mix(lhs, block[:, 256 * q : 256 * q + 256])
    for h in range(2):
        stacked = jnp.concatenate(
            [grams[t, 32 * h : 32 * h + 32, 256 * q : 256 * q + 256] for t in range(2) for q in range(4)], axis=0
        )
        zout[256 * h : 256 * h + 256, :] = mix(perm[GRAMS_OUT], stacked)
    zg = Column(zout, zin, zg_sem, (z, chip, c))
    zg.start()

    rspread.middle()
    scaled = jnp.concatenate([mix(lsel[...], block[:, 256 * q : 256 * q + 256]) for q in range(4)], axis=1)
    rspread.end()
    for n in range(4):
        turned = mix(perm[RIGHT_ROWS], rheld[256 * n : 256 * n + 256, :])
        for zz in range(PLANES):
            rfull[64 * zz + 16 * n : 64 * zz + 16 * n + 16, :] = turned[16 * zz : 16 * zz + 16]
    for q in range(4):
        grams[0, :, 256 * q : 256 * q + 256] = mix(scaled, rfull[:, 256 * q : 256 * q + 256])
    for h in range(2):
        stacked = jnp.concatenate(
            [grams[0, 32 * h : 32 * h + 32, 128 * n : 128 * n + 128] for n in range(8)], axis=0
        )
        pout[256 * h : 256 * h + 256, :] = mix(perm[SCALED_OUT], stacked)
    zp = Column(pout, pin, zp_sem, (z, chip, c))
    zp.start()

    zg.wait(1)
    stats_out[...] = mix(to_places[...], zin[...])
    f = Plane(stats_out, stats_in, f_sem, (z, o))
    f.start()

    zp.wait(1)
    for h in range(2):
        turned = mix(perm[T16], pin[256 * h : 256 * h + 256, :])
        for n in range(16):
            precond_ref[16 * h : 16 * h + 16, 128 * n : 128 * n + 128] = turned[16 * n : 16 * n + 16]

    loads[3].wait()
    loads[4].wait()
    f.wait(1)
    for k in range(4):
        turned = jnp.dot(perm[STATS_IN], stats_in[256 * k : 256 * k + 256, :], preferred_element_type=F32)
        for p in range(2):
            for t, (old, new) in enumerate(((lstat, left_ref), (rstat, right_ref))):
                for q in range(4):
                    at = ((p * 2 + t) * 4 + q) * 16
                    there = (p, slice(16 * k, 16 * k + 16), slice(256 * q, 256 * q + 256))
                    new[there] = decay_rate * old[there] + (1.0 - decay_rate) * turned[at : at + 16]

    for held, steps in ((from_left, 8), (from_right, 7)):
        ref = held.at[pl.ds(0, steps)]
        pltpu.make_async_copy(ref, ref, rs_send).wait()
    swap_copy(o).wait_send()
    spread.sent()
    rspread.sent()
    for exchange in (a1, a2, zg, zp, f):
        exchange.wait(0)


def step(grad_partials, block_owner, block_slot, left_stat, right_stat, left_root, right_root):
    vmem = pl.BlockSpec(memory_space=pltpu.VMEM)
    smem = pl.BlockSpec(memory_space=pltpu.SMEM)
    hbm = pl.BlockSpec(memory_space=pl.ANY)
    dma = pltpu.SemaphoreType.DMA
    return pl.pallas_call(
        kernel,
        out_shape=(
            jax.ShapeDtypeStruct((BLOCKS, 2 * WIDTH), BF16),
            jax.ShapeDtypeStruct(left_stat.shape, F32),
            jax.ShapeDtypeStruct(right_stat.shape, F32),
        ),
        in_specs=[smem, smem] + [hbm] * 5,
        out_specs=[vmem] * 3,
        scratch_shapes=[
            pltpu.VMEM((32, 32 * WIDTH), BF16),
            pltpu.VMEM((2, 64, WIDTH), F32),
            pltpu.VMEM((2, 64, WIDTH), F32),
            pltpu.VMEM((2, 64, WIDTH), BF16),
            pltpu.VMEM((2, 64, WIDTH), BF16),
            pltpu.VMEM((7, 256, 256), BF16),
            pltpu.VMEM((16, 64, WIDTH), BF16),
            pltpu.VMEM((8, 64, WIDTH), BF16),
            pltpu.VMEM((7, 64, WIDTH), BF16),
            pltpu.VMEM((32, WIDTH), BF16),
            pltpu.VMEM((WIDTH, WIDTH), BF16),
            pltpu.VMEM((1024, 256), BF16),
            pltpu.VMEM((1024, 256), BF16),
            pltpu.VMEM((512, 256), BF16),
            pltpu.VMEM((512, 256), BF16),
            pltpu.VMEM((64, WIDTH), BF16),
            pltpu.VMEM((WIDTH, WIDTH), BF16),
            pltpu.VMEM((WIDTH, WIDTH), BF16),
            pltpu.VMEM((2, 64, WIDTH), BF16),
            pltpu.VMEM((512, 256), BF16),
            pltpu.VMEM((512, 256), BF16),
            pltpu.VMEM((1024, 256), BF16),
            pltpu.VMEM((1024, 256), BF16),
            pltpu.VMEM((512, 128), BF16),
            pltpu.VMEM((512, 128), BF16),
            pltpu.VMEM((512, 1024), BF16),
            pltpu.VMEM((1024, 512), BF16),
            dma((5,)),
            dma,
            dma((8, SUBS)),
            dma((7, SUBS)),
            dma((2,)),
            dma,
            dma((2, 4, 4, 2)),
            dma,
            dma((2, 4, 4, 2)),
            dma((2,)),
            dma((2,)),
            dma((2,)),
            dma((2,)),
            dma((2,)),
        ],
        compiler_params=pltpu.CompilerParams(
            collective_id=0, has_side_effects=True, vmem_limit_bytes=44 * 1024 * 1024
        ),
    )(block_owner, block_slot, grad_partials, left_stat, right_stat, left_root, right_root)


def solution(mesh):
    return jax.shard_map(
        step,
        mesh=mesh,
        in_specs=(
            P("dp", None, "owner"),
            P(),
            P(),
            P("owner", "dp", None),
            P("owner", "dp", None),
            P("owner", "dp", None),
            P("owner", "dp", None),
        ),
        out_specs=(P(None, ("dp", "owner")), P("owner", "dp", None), P("owner", "dp", None)),
        check_vma=False,
    )
```

time: 278 us -> 110 us (0.40)
  waiting for transfers between devices: 200 us -> 0 us
  Pallas kernels: 0 us -> 99.8 us
  starting transfers between devices: 23.6 us -> 0 us
  matrix products: 17.6 us -> 0 us
  between operations: 14.1 us -> 0.66 us
  local copies, waits for them, and re-layouts: 21.4 us -> 9.12 us
    psum x1 -> x0, waiting for transfers between devices: 142 us -> none  [shards(): summed = lax.psum(summands.astype(jnp.bfloat16), 'dp')]
    pallas_call x0 -> x1, Pallas kernels: none -> 99.8 us  [step(): pl.pallas_call(kernel, out_shape=(jax.ShapeDtypeStruct((BLOCKS, 2 * WIDTH...]
    all_to_all x2 -> x0, waiting for transfers between devices: 56.7 us -> none  [the longest x1 52.2 us: shards(): lax.all_to_all(packed, 'owner', split_axis=1, concat_axis=1, tiled=True)]
    all_to_all x2 -> x0, starting transfers between devices: 23.6 us -> none  [the longest x1 16.4 us: shards(): lax.all_to_all(packed, 'owner', split_axis=1, concat_axis=1, tiled=True)]
    dot_general x5 -> x0, matrix products: 17.6 us -> none  [the longest x1 5.09 us: shards(): jnp.einsum('qrk,qkc->qrc', scaled, lax.all_gather(right_root, 'dp', axis=...]
    reshape x4 -> x0, local copies, waits for them, and re-layouts: 14.9 us -> none  [the longest x1 7.53 us: shards(): blocks = arrived.reshape(capacity, block_width, block_width)]
    unnamed x6 -> x17, local copies, waits for them, and re-layouts: 0.02 us -> 9.12 us
    all_to_all x2 -> x0, local copies, waits for them, and re-layouts: 6.54 us -> none  [the longest x1 6.46 us: shards(): lax.all_to_all(packed, 'owner', split_axis=1, concat_axis=1, tiled=True)]
  transfers between devices with their start and end apart: 4 -> 0, of which waited for: 3 -> 0; matrix products, arithmetic and copies ran while one was open for 12% -> 0% of each run, Pallas kernels for 0% -> 0%
where the time goes in v1:
time: 110 us
  Pallas kernels  99.8 us (91%)
  local copies, waits for them, and re-layouts  9.12 us (8%)
    pallas_call x1, Pallas kernels, step(): pl.pallas_call(kernel, out_shape=(jax.ShapeDtypeStruct((BLOCKS, 2 * WIDTH...  99.8 us
    unnamed x17, local copies, waits for them, and re-layouts  9.12 us

profile of v1, /device:TPU:1, one launch (start us, length us, event | category | flops | bytes accessed | tf_op | source)
XLA Modules:
  0.0 109.6 jit_solution(4479949397752701939)
XLA Ops:
  0.6 0.0 copy-start
  0.6 1.6 %copy-done = bf16[1,32,32768]{2,1,0:T(8,128)(2,1)S(1)} copy-done((bf16[1,32,32768]{2,1,0:T(8,128)(2,1)S(1)}, bf16[1,32,32768]{2,1,0:T(8,128)(2,1)}, u32[]{:S(2)}) %copy-start) | copy-done | bytes 2097176
  2.2 0.0 copy-start.1
  2.2 1.0 copy-done.1
  3.3 0.0 copy-start.2
  3.3 1.0 copy-done.2
  4.3 0.0 copy-start.3
  4.3 0.9 copy-done.3
  5.3 0.0 copy-start.4
  5.3 0.9 copy-done.4
  6.2 0.0 copy-start.5
  6.2 0.7 copy-done.5
  6.9 0.0 copy-start.6
  6.9 0.7 copy-done.6
  7.5 99.8 %shard_map.94 = (bf16[32,2048]{1,0:T(8,128)(2,1)S(1)}, f32[2,64,1024]{2,1,0:T(8,128)S(1)}, f32[2,64,1024]{2,1,0:T(8,128)S(1)}) custom-call(s32[32]{0:T(128)S(1)} %copy-done.5, s32[32]{0:T(128)S(1)} %copy-done.6, bf16[1,32,32768]{2,1,0:T(8,128)(2,1)S(1)} %copy-done, f32[2,64,1024]{2,1,0:T(8,128)S(1)} %copy-done.1, f32[2,64,1024]{2,1,0:T(8,128)S(1)} %copy-done.2, ...), custom_call_target="tpu_custom_call" | custom-call | tf_op jit(solution)/shard_map/pallas_call | solution.py:449
  107.3 0.7 copy.13
  108.0 0.8 copy.14
  108.8 0.8 copy.15
Async XLA Ops:
  0.6 1.6 %copy-start = (bf16[1,32,32768]{2,1,0:T(8,128)(2,1)S(1)}, bf16[1,32,32768]{2,1,0:T(8,128)(2,1)}, u32[]{:S(2)}) copy-start(bf16[1,32,32768]{2,1,0:T(8,128)(2,1)} %g_hbm.1) | copy-start | bytes 6291460
  2.2 1.0 copy-start.1
  3.3 1.0 copy-start.2
  4.3 0.9 copy-start.3
  5.3 0.9 copy-start.4
  6.2 0.7 copy-start.5
  6.9 0.7 copy-start.6

commit v2 on v1

v2 whole, which is shorter than its diff:
```python
import functools

import jax
import jax.numpy as jnp
from jax import lax
from jax.experimental import pallas as pl
from jax.experimental.pallas import tpu as pltpu
from jax.sharding import PartitionSpec as P

decay_rate = 0.95

MESH = pl.DeviceIdType.MESH
BF16 = jnp.bfloat16
F32 = jnp.float32
PLANES = 16
OWNERS = 32
BLOCKS = 32
WIDTH = 1024
SUBS = 4


def iotas(rows, columns):
    return (
        lax.broadcasted_iota(jnp.int32, (rows, columns), 0),
        lax.broadcasted_iota(jnp.int32, (rows, columns), 1),
    )


def one_hot(hit):
    return jnp.where(hit, 1.0, 0.0).astype(BF16)


def mix(chooser, data):
    return jnp.dot(chooser, data, preferred_element_type=F32).astype(BF16)


def times_transposed(a, b):
    return lax.dot_general(a, b, (((1,), (1,)), ((), ())), preferred_element_type=F32)


def chunk(start, size, unit=None):
    return pl.ds(pl.multiple_of(start, unit or size), size)


def transpose16(m):
    return (m % 16) * 16 + m // 16


def roots_out(m):
    return (((m >> 4) & 1) * 32 + ((m >> 3) & 1) * 16 + (m & 3) * 4) * 4 + (m >> 5) * 2 + ((m >> 2) & 1)


def roots_in(m):
    return ((m >> 1) & 15) * 16 + (m >> 7) * 8 + (m & 1) * 4 + ((m >> 5) & 3)


def results_out(m):
    return ((m & 7) * 16 + (m >> 4)) * 2 + ((m >> 3) & 1)


def right_rows(m):
    return ((m >> 2) & 3) * 64 + (m >> 4) * 4 + (m & 3)


def stats_in(m):
    return ((m >> 1) & 7) * 32 + (m >> 7) * 16 + (m & 1) * 8 + ((m >> 4) & 7)


def shuffle(source):
    m, k = iotas(256, 256)
    return one_hot(k == source(m))


SHUFFLES = (transpose16, roots_out, roots_in, results_out, right_rows)
T16, ROOTS_OUT, ROOTS_IN, RESULTS_OUT, RIGHT_ROWS = range(5)


class Spread:
    def __init__(self, buf, send_sem, recv_sem, place):
        self.buf, self.send_sem, self.recv_sem = buf, send_sem, recv_sem
        self.z, self.x, self.y, self.c = place

    def chip(self, h, da, db):
        first, second = (self.x, self.y) if h == 0 else (self.y, self.x)
        first, second = (first + da) % 4, (second + db) % 4
        return (first, second) if h == 0 else (second, first)

    def piece(self, h, da, db, half=None):
        px, py = self.chip(h, da, db)
        start = px * 256 + py * 64 + (self.c if h == 0 else 1 - self.c) * 32
        if half is None:
            return self.buf.at[chunk(start, 32)]
        return self.buf.at[chunk(start + 16 * half, 16)]

    def copy(self, h, da, db, half, axis, delta):
        px, py = self.chip(h, delta if axis == 0 else 0, delta if axis == 1 else 0)
        there = ((da - delta) % 4, db) if axis == 0 else (da, (db - delta) % 4)
        ref = self.piece(h, da, db, half)
        return pltpu.make_async_remote_copy(
            src_ref=ref,
            dst_ref=ref,
            send_sem=self.send_sem,
            recv_sem=self.recv_sem.at[h, there[0], there[1], half or 0],
            device_id=(self.z, (px * 4 + py) * 2 + self.c),
            device_id_type=MESH,
        )

    def wait(self, h, da, db, half=None):
        ref = self.piece(h, da, db, half)
        pltpu.make_async_copy(ref, ref, self.recv_sem.at[h, da, db, half or 0]).wait()

    def across(self, h, da):
        for delta in (1, -1):
            self.copy(h, da, 0, None, 1, delta).start()

    def begin(self, h):
        for delta in (1, -1):
            self.copy(h, 0, 0, None, 0, delta).start()
        self.across(h, 0)

    def middle(self):
        for da, half, delta in ((3, 0, 1), (1, 1, -1)):
            for h in (0, 1):
                self.wait(h, da, 0)
                self.copy(h, da, 0, half, 0, delta).start()
                self.across(h, da)
        self.turn(0)
        for h in (0, 1):
            self.wait(h, 2, 0, 0)
            self.wait(h, 2, 0, 1)
            self.across(h, 2)
        self.turn(3)
        self.turn(1)
        self.turn(2)

    def turn(self, da):
        for db, half, delta in ((3, 0, 1), (1, 1, -1)):
            for h in (0, 1):
                self.wait(h, da, db)
                self.copy(h, da, db, half, 1, delta).start()

    def end(self):
        for da in (0, 3, 1, 2):
            for h in (0, 1):
                self.wait(h, da, 2, 0)
                self.wait(h, da, 2, 1)

    def sent(self):
        ref = self.buf.at[pl.ds(0, 960)]
        pltpu.make_async_copy(ref, ref, self.send_sem).wait()


class Column:
    def __init__(self, src, dst, sems, place):
        self.src, self.dst, self.sems = src, dst, sems
        self.z, self.chip, self.c = place

    def copy(self, zd, e):
        return pltpu.make_async_remote_copy(
            src_ref=self.src.at[chunk((2 * zd + e) * 16, 16)],
            dst_ref=self.dst.at[chunk((2 * self.z + self.c) * 16, 16)],
            send_sem=self.sems.at[0],
            recv_sem=self.sems.at[1],
            device_id=(zd, 2 * self.chip + e),
            device_id_type=MESH,
        )

    def start(self):
        def step(j, carry):
            for zd in ((self.z + PLANES // 2 - j) % PLANES, (self.z + PLANES // 2 + j) % PLANES):
                for e in (0, 1):
                    self.copy(zd, e).start()
            return carry

        for e in (0, 1):
            self.copy((self.z + PLANES // 2) % PLANES, e).start()
        lax.fori_loop(1, PLANES // 2, step, 0)
        self.copy(self.z, 1 - self.c).start()
        own = chunk((2 * self.z + self.c) * 16, 16)
        self.dst[own, :] = self.src[own, :]

    def wait(self, which):
        ref = self.dst.at[pl.ds(0, 31 * 16)]
        pltpu.make_async_copy(ref, ref, self.sems.at[which]).wait()


FAR_FIRST = sorted(
    ((dx, dy, dc) for dx in range(4) for dy in range(4) for dc in range(2) if (dx, dy, dc) != (0, 0, 0)),
    key=lambda d: -min(d[0], 4 - d[0]) - min(d[1], 4 - d[1]),
)


class Plane:
    def __init__(self, src, dst, sems, place):
        self.src, self.dst, self.sems = src, dst, sems
        self.z, self.o = place

    def start(self):
        x, y, c = self.o // 8, self.o // 2 % 4, self.o % 2
        for dx, dy, dc in FAR_FIRST:
            there = (((x + dx) % 4) * 4 + (y + dy) % 4) * 2 + (c + dc) % 2
            pltpu.make_async_remote_copy(
                src_ref=self.src.at[chunk(there * 32, 32)],
                dst_ref=self.dst.at[chunk(self.o * 32, 32)],
                send_sem=self.sems.at[0],
                recv_sem=self.sems.at[1],
                device_id=(self.z, there),
                device_id_type=MESH,
            ).start()
        own = chunk(self.o * 32, 32)
        self.dst[own, :] = self.src[own, :]

    def wait(self, which):
        ref = self.dst.at[pl.ds(0, 31 * 32)]
        pltpu.make_async_copy(ref, ref, self.sems.at[which]).wait()


def kernel(
    owner_hbm, slot_hbm, g_hbm, lroot_hbm, rroot_hbm,
    arrived_ref,
    owner_ref, slot_ref, g, lroot, rroot, perm, parts, from_left, from_right, swapped, block,
    roots_out, roots_in, blocks_out, blocks_in, lsel, rheld, rfull,
    rows64, zout, zin, stats_out, stats_held, to_blocks, to_places,
    load_sem, near_sem, rs_send, right_sem, left_sem, swap_sem, block_send, block_recv, rheld_send, rheld_recv,
    a1_sem, a2_sem, z_sem, f_sem,
):
    z, o = lax.axis_index("dp"), lax.axis_index("owner")
    chip, c = o // 2, o % 2
    x, y = chip // 4, chip % 4

    loads = [
        pltpu.make_async_copy(src, dst, load_sem.at[n])
        for n, (src, dst) in enumerate(
            ((g_hbm.at[0], g), (lroot_hbm, lroot), (rroot_hbm, rroot), (owner_hbm, owner_ref), (slot_hbm, slot_ref))
        )
    ]
    for load in loads:
        load.start()

    def core_of(dx, dy, dc):
        return (z, (((x + dx) % 4) * 4 + (y + dy) % 4) * 2 + (c + dc) % 2)

    barrier = pltpu.get_barrier_semaphore()
    along_x = [core_of(d, 0, dc) for d in (1, 2, 3) for dc in (0, 1)]
    along_y = [core_of(0, d, dc) for d in (1, 2, 3) for dc in (0, 1)]
    greeted = [((z + 1) % PLANES, o), ((z + PLANES - 1) % PLANES, o), core_of(0, 0, 1)] + along_x + along_y
    for there in greeted:
        pl.semaphore_signal(barrier, inc=1, device_id=there, device_id_type=MESH)

    for n, source in enumerate(SHUFFLES):
        perm[n] = shuffle(source)

    loads[0].wait()
    for h in range(2):
        for q in range(2):
            for w in range(4):
                columns = [(16 * q + r) * WIDTH + 256 * w for r in range(16)]
                stacked = jnp.concatenate([g[16 * h : 16 * h + 16, n : n + 256] for n in columns], axis=0)
                turned = mix(perm[T16], stacked)
                for b in range(16):
                    at = (b % 2) * 32 + 16 * q
                    parts[8 * h + b // 2, at : at + 16, 256 * w : 256 * w + 256] = turned[16 * b : 16 * b + 16]

    pl.semaphore_wait(barrier, len(greeted))

    def rs_copy(right, s, sub):
        rows = pl.ds(sub * 16, 16)
        held = from_left if right else from_right
        part = (z + 8 - s) % PLANES if right else (z + 8 + s) % PLANES
        sems = right_sem if right else left_sem
        return pltpu.make_async_remote_copy(
            src_ref=parts.at[part, rows] if s == rs_first(right, sub) else held.at[s - 1, rows],
            dst_ref=held.at[s, rows],
            send_sem=rs_send,
            recv_sem=sems.at[s, sub],
            device_id=((z + (1 if right else PLANES - 1)) % PLANES, o),
            device_id_type=MESH,
        )

    def rs_first(right, sub):
        return 0 if (sub < SUBS // 2) == right else 1

    def rs_step(s):
        for sub in range(SUBS):
            for right in (True, False):
                if s < rs_first(right, sub):
                    continue
                if s > rs_first(right, sub):
                    rs_copy(right, s - 1, sub).wait_recv()
                    rows = pl.ds(sub * 16, 16)
                    held = from_left if right else from_right
                    part = (z + 8 - s) % PLANES if right else (z + 8 + s) % PLANES
                    total = held[s - 1, rows, :].astype(F32) + parts[part, rows, :].astype(F32)
                    held[s - 1, rows, :] = total.astype(BF16)
                rs_copy(right, s, sub).start()

    rs_step(0)
    rs_step(1)

    for there in along_x:
        pl.semaphore_signal(near_sem, inc=1, device_id=there, device_id_type=MESH)
    loads[1].wait()
    loads[2].wait()
    for k in range(4):
        stacked = jnp.concatenate(
            [
                root[p, 16 * k : 16 * k + 16, 256 * q : 256 * q + 256]
                for p in range(2)
                for root in (lroot, rroot)
                for q in range(4)
            ],
            axis=0,
        )
        roots_out[256 * k : 256 * k + 256, :] = mix(perm[ROOTS_OUT], stacked)
    pl.semaphore_wait(near_sem, len(along_x))
    a1 = Plane(roots_out, roots_in, a1_sem, (z, o))
    a1.start()

    rs_step(2)

    loads[3].wait()
    loads[4].wait()
    places = [owner_ref[b] * 2 + slot_ref[b] for b in range(BLOCKS)]
    row, column = iotas(16, WIDTH)
    for b in range(BLOCKS):
        to_blocks[16 * b : 16 * b + 16, :] = one_hot(column == places[b] * 16 + row)
    column = lax.broadcasted_iota(jnp.int32, (1, 512), 1)
    target = jnp.zeros((1, 512), jnp.int32)
    for b in range(BLOCKS):
        target = jnp.where(column // 16 == b, places[b] * 16, target)
    target = target + column % 16
    for k in range(4):
        row = lax.broadcasted_iota(jnp.int32, (256, 512), 0) + 256 * k
        to_places[256 * k : 256 * k + 256, :] = one_hot(row == target)

    rs_step(3)
    rs_step(4)
    rs_step(5)

    a1.wait(1)
    blocks_out[...] = mix(to_blocks[...], roots_in[...])

    rs_step(6)
    rs_step(7)

    def last_sum(which):
        rows = chunk(which * 32, 32)
        for held, sems in ((from_left, right_sem), (from_right, left_sem)):
            for n in range(2):
                ref = held.at[7, chunk(which * 32 + n * 16, 16)]
                pltpu.make_async_copy(ref, ref, sems.at[7, which * 2 + n]).wait()
        total = parts[z, rows, :].astype(F32) + from_left[7, rows, :].astype(F32) + from_right[7, rows, :].astype(F32)
        return total.astype(BF16)

    def swap_copy(rows_of):
        return pltpu.make_async_remote_copy(
            src_ref=swapped,
            dst_ref=block.at[chunk(rows_of * 32, 32)],
            send_sem=swap_sem.at[0],
            recv_sem=swap_sem.at[1],
            device_id=(z, 2 * chip + 1 - c),
            device_id_type=MESH,
        )

    swapped[...] = last_sum(1 - c)
    swap_copy(o).start()
    block[chunk(o * 32, 32), :] = last_sum(c)
    spread = Spread(block, block_send, block_recv, (z, x, y, c))
    spread.begin(0)
    swap_copy(2 * chip + 1 - c).wait_recv()
    spread.begin(1)
    a2 = Column(blocks_out, blocks_in, a2_sem, (z, chip, c))
    a2.start()
    spread.middle()

    a2.wait(1)
    for h in range(2):
        turned = mix(perm[ROOTS_IN], blocks_in[256 * h : 256 * h + 256, :])
        for q in range(4):
            lsel[32 * h : 32 * h + 32, 256 * q : 256 * q + 256] = turned[32 * q : 32 * q + 32]
            rheld[chunk(chip * 64 + 32 * h, 32), 256 * q : 256 * q + 256] = turned[128 + 32 * q : 160 + 32 * q]
    rspread = Spread(rheld, rheld_send, rheld_recv, (z, x, y, c))
    rspread.begin(0)
    rspread.begin(1)

    spread.end()

    def send_rows(n, product):
        for q in range(4):
            rows64[n, :, 256 * q : 256 * q + 256] = product(q).astype(BF16)
        for h in range(2):
            stacked = jnp.concatenate(
                [rows64[n, 32 * h : 32 * h + 32, 128 * q : 128 * q + 128] for q in range(8)], axis=0
            )
            zout[n, 256 * h : 256 * h + 256, :] = mix(perm[RESULTS_OUT], stacked)
        exchange = Column(zout.at[n], zin.at[n], z_sem.at[n], (z, chip, c))
        exchange.start()
        return exchange

    m, k = iotas(64, 256)
    chosen = one_hot(k == (m >> 2) * 16 + 4 * y + (m & 3))
    stacked = jnp.concatenate([block[chunk(64 * zz + 16 * x, 16), :] for zz in range(PLANES)], axis=0)
    lhs = mix(chosen, stacked)
    zl = send_rows(0, lambda q: times_transposed(lhs, block[256 * q : 256 * q + 256, :]))
    m, k = iotas(64, WIDTH)
    chosen = one_hot(k == (m >> 2) * 64 + 4 * chip + (m & 3))
    columns = jnp.concatenate(
        [times_transposed(chosen, block[256 * q : 256 * q + 256, :]).astype(BF16) for q in range(4)], axis=1
    )
    zr = send_rows(1, lambda q: jnp.dot(columns, block[:, 256 * q : 256 * q + 256], preferred_element_type=F32))

    rspread.middle()
    scaled = jnp.concatenate([mix(lsel[...], block[:, 256 * q : 256 * q + 256]) for q in range(4)], axis=1)

    def to_owners(n, exchange):
        exchange.wait(1)
        stats_out[n] = mix(to_places[...], zin[n])
        owners = Plane(stats_out.at[n], stats_held.at[n], f_sem.at[n], (z, o))
        owners.start()
        return owners

    fl = to_owners(0, zl)

    rspread.end()
    for n in range(4):
        turned = mix(perm[RIGHT_ROWS], rheld[256 * n : 256 * n + 256, :])
        for zz in range(PLANES):
            rfull[64 * zz + 16 * n : 64 * zz + 16 * n + 16, :] = turned[16 * zz : 16 * zz + 16]
    zp = send_rows(2, lambda q: jnp.dot(scaled, rfull[:, 256 * q : 256 * q + 256], preferred_element_type=F32))

    fr = to_owners(1, zr)

    fl.wait(1)
    stores = [pltpu.make_async_copy(stats_held.at[0], arrived_ref.at[pl.ds(0, 1024)], load_sem.at[0])]
    stores[0].start()
    fr.wait(1)
    stores.append(pltpu.make_async_copy(stats_held.at[1], arrived_ref.at[pl.ds(1024, 1024)], load_sem.at[1]))
    stores[1].start()
    zp.wait(1)
    stores.append(pltpu.make_async_copy(zin.at[2], arrived_ref.at[pl.ds(2048, 512)], load_sem.at[2]))
    stores[2].start()

    ref = parts.at[pl.ds(0, 15)]
    pltpu.make_async_copy(ref, ref, rs_send).wait()
    swap_copy(o).wait_send()
    spread.sent()
    rspread.sent()
    for exchange in (a1, a2, zl, zr, zp, fl, fr):
        exchange.wait(0)
    for store in stores:
        store.wait()


def finish(arrived_ref, lstat_ref, rstat_ref, precond_ref, left_ref, right_ref):
    turn = shuffle(transpose16)
    for h in range(2):
        turned = mix(turn, arrived_ref[2048 + 256 * h : 2304 + 256 * h, :])
        for n in range(16):
            precond_ref[16 * h : 16 * h + 16, 128 * n : 128 * n + 128] = turned[16 * n : 16 * n + 16]
    turn = shuffle(stats_in)
    for t, (old, new) in enumerate(((lstat_ref, left_ref), (rstat_ref, right_ref))):
        for k in range(4):
            turned = jnp.dot(turn, arrived_ref[1024 * t + 256 * k : 1024 * t + 256 * k + 256, :], preferred_element_type=F32)
            for p in range(2):
                for n in range(8):
                    at = (p * 8 + n) * 16
                    there = (p, slice(16 * k, 16 * k + 16), slice(128 * n, 128 * n + 128))
                    new[there] = decay_rate * old[there] + (1.0 - decay_rate) * turned[at : at + 16]


def step(grad_partials, block_owner, block_slot, left_stat, right_stat, left_root, right_root):
    vmem = pl.BlockSpec(memory_space=pltpu.VMEM)
    hbm = pl.BlockSpec(memory_space=pl.ANY)
    dma = pltpu.SemaphoreType.DMA
    arrived = pl.pallas_call(
        kernel,
        out_shape=jax.ShapeDtypeStruct((2560, 128), BF16),
        in_specs=[hbm] * 5,
        out_specs=hbm,
        scratch_shapes=[
            pltpu.SMEM((BLOCKS,), jnp.int32),
            pltpu.SMEM((BLOCKS,), jnp.int32),
            pltpu.VMEM((32, 32 * WIDTH), BF16),
            pltpu.VMEM((2, 64, WIDTH), BF16),
            pltpu.VMEM((2, 64, WIDTH), BF16),
            pltpu.VMEM((len(SHUFFLES), 256, 256), BF16),
            pltpu.VMEM((16, 64, WIDTH), BF16),
            pltpu.VMEM((8, 64, WIDTH), BF16),
            pltpu.VMEM((8, 64, WIDTH), BF16),
            pltpu.VMEM((32, WIDTH), BF16),
            pltpu.VMEM((WIDTH, WIDTH), BF16),
            pltpu.VMEM((1024, 256), BF16),
            pltpu.VMEM((1024, 256), BF16),
            pltpu.VMEM((512, 256), BF16),
            pltpu.VMEM((512, 256), BF16),
            pltpu.VMEM((64, WIDTH), BF16),
            pltpu.VMEM((WIDTH, WIDTH), BF16),
            pltpu.VMEM((WIDTH, WIDTH), BF16),
            pltpu.VMEM((3, 64, WIDTH), BF16),
            pltpu.VMEM((3, 512, 128), BF16),
            pltpu.VMEM((3, 512, 128), BF16),
            pltpu.VMEM((2, 1024, 128), BF16),
            pltpu.VMEM((2, 1024, 128), BF16),
            pltpu.VMEM((512, 1024), BF16),
            pltpu.VMEM((1024, 512), BF16),
            dma((5,)),
            pltpu.SemaphoreType.REGULAR,
            dma,
            dma((8, SUBS)),
            dma((8, SUBS)),
            dma((2,)),
            dma,
            dma((2, 4, 4, 2)),
            dma,
            dma((2, 4, 4, 2)),
            dma((2,)),
            dma((2,)),
            dma((3, 2)),
            dma((2, 2)),
        ],
        compiler_params=pltpu.CompilerParams(
            collective_id=0, has_side_effects=True, vmem_limit_bytes=60 * 1024 * 1024
        ),
    )(block_owner, block_slot, grad_partials, left_root, right_root)
    return pl.pallas_call(
        finish,
        out_shape=(
            jax.ShapeDtypeStruct((BLOCKS, 2 * WIDTH), BF16),
            jax.ShapeDtypeStruct(left_stat.shape, F32),
            jax.ShapeDtypeStruct(right_stat.shape, F32),
        ),
        in_specs=[vmem] * 3,
        out_specs=[vmem] * 3,
        compiler_params=pltpu.CompilerParams(vmem_limit_bytes=16 * 1024 * 1024),
    )(arrived, left_stat, right_stat)


def solution(mesh):
    return jax.shard_map(
        step,
        mesh=mesh,
        in_specs=(
            P("dp", None, "owner"),
            P(),
            P(),
            P("owner", "dp", None),
            P("owner", "dp", None),
            P("owner", "dp", None),
            P("owner", "dp", None),
        ),
        out_specs=(P(None, ("dp", "owner")), P("owner", "dp", None), P("owner", "dp", None)),
        check_vma=False,
    )
```

time: 110 us -> 94.4 us (0.86)
  local copies, waits for them, and re-layouts: 9.12 us -> 1.09 us
  Pallas kernels: 99.8 us -> 92.4 us
    unnamed x17 -> x6, local copies, waits for them, and re-layouts: 9.12 us -> 1.09 us
    pallas_call x1 -> x2, Pallas kernels: 99.8 us -> 92.4 us  [the longest x1 91.1 us: step(): pl.pallas_call(kernel, out_shape=jax.ShapeDtypeStruct((2560, 128), BF16),...]
where the time goes in v2:
time: 94.4 us; the launch traced here: 94.2 us
  Pallas kernels  92.4 us (98%)
  local copies, waits for them, and re-layouts  1.09 us (1%)
    pallas_call x1, Pallas kernels, step(): pl.pallas_call(kernel, out_shape=jax.ShapeDtypeStruct((2560, 128), BF16),...  91.1 us

profile of v2, /device:TPU:1, one launch (start us, length us, event | category | flops | bytes accessed | tf_op | source)
XLA Modules:
  0.0 94.2 jit_solution(6103474754605416104)
XLA Ops:
  0.6 0.0 copy-start.2
  0.6 0.0 copy-start.1
  0.7 91.1 %shard_map.94.arrived_ref = bf16[2560,128]{1,0:T(8,128)(2,1)} custom-call(s32[32]{0:T(128)} %owner_hbm.1, s32[32]{0:T(128)} %slot_hbm.1, bf16[1,32,32768]{2,1,0:T(8,128)(2,1)} %g_hbm.1, bf16[2,64,1024]{2,1,0:T(8,128)(2,1)} %lroot_hbm.1, bf16[2,64,1024]{2,1,0:T(8,128)(2,1)} %rroot_hbm.1), custom_call_target="tpu_custom_call" | custom-call | tf_op jit(solution)/shard_map/pallas_call | solution.py:475
  91.8 0.0 copy-done.2
  91.8 0.0 copy-done.1
  91.8 0.0 copy-start
  91.8 1.1 %copy-done = bf16[2560,128]{1,0:T(8,128)(2,1)S(1)} copy-done((bf16[2560,128]{1,0:T(8,128)(2,1)S(1)}, bf16[2560,128]{1,0:T(8,128)(2,1)}, u32[]{:S(2)}) %copy-start) | copy-done | bytes 655384
  92.9 1.3 %shard_map.95 = (bf16[32,2048]{1,0:T(8,128)(2,1)}, f32[2,64,1024]{2,1,0:T(8,128)}, f32[2,64,1024]{2,1,0:T(8,128)}) custom-call(bf16[2560,128]{1,0:T(8,128)(2,1)S(1)} %copy-done, f32[2,64,1024]{2,1,0:T(8,128)S(1)} %copy-done.1, f32[2,64,1024]{2,1,0:T(8,128)S(1)} %copy-done.2), custom_call_target="tpu_custom_call" | custom-call | tf_op jit(solution)/shard_map/pallas_call | solution.py:525
Async XLA Ops:
  0.6 91.1 %copy-start.2 = (f32[2,64,1024]{2,1,0:T(8,128)S(1)}, f32[2,64,1024]{2,1,0:T(8,128)}, u32[]{:S(2)}) copy-start(f32[2,64,1024]{2,1,0:T(8,128)} %rstat_ref.1) | copy-start | bytes 1572868
  0.6 91.1 %copy-start.1 = (f32[2,64,1024]{2,1,0:T(8,128)S(1)}, f32[2,64,1024]{2,1,0:T(8,128)}, u32[]{:S(2)}) copy-start(f32[2,64,1024]{2,1,0:T(8,128)} %lstat_ref.1) | copy-start | bytes 1572868
  91.8 1.1 %copy-start = (bf16[2560,128]{1,0:T(8,128)(2,1)S(1)}, bf16[2560,128]{1,0:T(8,128)(2,1)}, u32[]{:S(2)}) copy-start(bf16[2560,128]{1,0:T(8,128)(2,1)} %shard_map.94.arrived_ref) | copy-start | bytes 1966084

commit v3 on v2

--- a/solution.py
+++ b/solution.py
@@ -47,19 +47,15 @@
 
 
 def roots_out(m):
-    return (((m >> 4) & 1) * 32 + ((m >> 3) & 1) * 16 + (m & 3) * 4) * 4 + (m >> 5) * 2 + ((m >> 2) & 1)
-
-
-def roots_in(m):
-    return ((m >> 1) & 15) * 16 + (m >> 7) * 8 + (m & 1) * 4 + ((m >> 5) & 3)
+    return (((m >> 4) & 1) * 8 + (m & 7)) * 16 + (m >> 5) * 2 + ((m >> 3) & 1)
+
+
+def results_in(m):
+    return ((m >> 1) & 15) * 16 + (m & 1) * 8 + (m >> 5)
 
 
 def results_out(m):
     return ((m & 7) * 16 + (m >> 4)) * 2 + ((m >> 3) & 1)
-
-
-def right_rows(m):
-    return ((m >> 2) & 3) * 64 + (m >> 4) * 4 + (m & 3)
 
 
 def stats_in(m):
@@ -71,8 +67,8 @@
     return one_hot(k == source(m))
 
 
-SHUFFLES = (transpose16, roots_out, roots_in, results_out, right_rows)
-T16, ROOTS_OUT, ROOTS_IN, RESULTS_OUT, RIGHT_ROWS = range(5)
+SHUFFLES = (transpose16, roots_out, results_in, results_out)
+T16, ROOTS_OUT, RESULTS_IN, RESULTS_OUT = range(4)
 
 
 class Spread:
@@ -118,20 +114,24 @@
             self.copy(h, 0, 0, None, 0, delta).start()
         self.across(h, 0)
 
-    def middle(self):
+    def early(self):
         for da, half, delta in ((3, 0, 1), (1, 1, -1)):
             for h in (0, 1):
                 self.wait(h, da, 0)
                 self.copy(h, da, 0, half, 0, delta).start()
                 self.across(h, da)
+
+    def middle(self):
         self.turn(0)
         for h in (0, 1):
             self.wait(h, 2, 0, 0)
             self.wait(h, 2, 0, 1)
+            self.copy(h, 2, 0, None, 1, 2).start()
             self.across(h, 2)
+
+    def late(self):
         self.turn(3)
         self.turn(1)
-        self.turn(2)
 
     def turn(self, da):
         for db, half, delta in ((3, 0, 1), (1, 1, -1)):
@@ -140,10 +140,13 @@
                 self.copy(h, da, db, half, 1, delta).start()
 
     def end(self):
-        for da in (0, 3, 1, 2):
+        for da in (0, 3, 1):
             for h in (0, 1):
                 self.wait(h, da, 2, 0)
                 self.wait(h, da, 2, 1)
+        for db in (3, 1, 2):
+            for h in (0, 1):
+                self.wait(h, 2, db)
 
     def sent(self):
         ref = self.buf.at[pl.ds(0, 960)]
@@ -219,8 +222,8 @@
     owner_hbm, slot_hbm, g_hbm, lroot_hbm, rroot_hbm,
     arrived_ref,
     owner_ref, slot_ref, g, lroot, rroot, perm, parts, from_left, from_right, swapped, block,
-    roots_out, roots_in, blocks_out, blocks_in, lsel, rheld, rfull,
-    rows64, zout, zin, stats_out, stats_held, to_blocks, to_places,
+    roots_out, roots_in, blocks_out, blocks_in, lsel, rheld, order,
+    rows64, zout, zin, stats_out, to_blocks, to_places,
     load_sem, near_sem, rs_send, right_sem, left_sem, swap_sem, block_send, block_recv, rheld_send, rheld_recv,
     a1_sem, a2_sem, z_sem, f_sem,
 ):
@@ -228,15 +231,6 @@
     chip, c = o // 2, o % 2
     x, y = chip // 4, chip % 4
 
-    loads = [
-        pltpu.make_async_copy(src, dst, load_sem.at[n])
-        for n, (src, dst) in enumerate(
-            ((g_hbm.at[0], g), (lroot_hbm, lroot), (rroot_hbm, rroot), (owner_hbm, owner_ref), (slot_hbm, slot_ref))
-        )
-    ]
-    for load in loads:
-        load.start()
-
     def core_of(dx, dy, dc):
         return (z, (((x + dx) % 4) * 4 + (y + dy) % 4) * 2 + (c + dc) % 2)
 
@@ -247,20 +241,31 @@
     for there in greeted:
         pl.semaphore_signal(barrier, inc=1, device_id=there, device_id_type=MESH)
 
-    for n, source in enumerate(SHUFFLES):
-        perm[n] = shuffle(source)
-
-    loads[0].wait()
-    for h in range(2):
+    first_half = (z + 8) % PLANES // 8
+    halves = [chunk(16 * h, 16) for h in (first_half, 1 - first_half)]
+    loads = [
+        pltpu.make_async_copy(src, dst, load_sem.at[n])
+        for n, (src, dst) in enumerate(
+            ((g_hbm.at[0, halves[0]], g.at[halves[0]]), (g_hbm.at[0, halves[1]], g.at[halves[1]]), (lroot_hbm, lroot), (rroot_hbm, rroot), (owner_hbm, owner_ref), (slot_hbm, slot_ref))
+        )
+    ]
+    for load in loads:
+        load.start()
+
+    perm[T16] = shuffle(transpose16)
+
+    def make_parts(h):
         for q in range(2):
             for w in range(4):
                 columns = [(16 * q + r) * WIDTH + 256 * w for r in range(16)]
-                stacked = jnp.concatenate([g[16 * h : 16 * h + 16, n : n + 256] for n in columns], axis=0)
+                stacked = jnp.concatenate([g[chunk(16 * h, 16), n : n + 256] for n in columns], axis=0)
                 turned = mix(perm[T16], stacked)
                 for b in range(16):
                     at = (b % 2) * 32 + 16 * q
                     parts[8 * h + b // 2, at : at + 16, 256 * w : 256 * w + 256] = turned[16 * b : 16 * b + 16]
 
+    loads[0].wait()
+    make_parts(first_half)
     pl.semaphore_wait(barrier, len(greeted))
 
     def rs_copy(right, s, sub):
@@ -295,31 +300,31 @@
                 rs_copy(right, s, sub).start()
 
     rs_step(0)
+    loads[1].wait()
+    make_parts(1 - first_half)
     rs_step(1)
+    for n, source in enumerate(SHUFFLES[1:]):
+        perm[n + 1] = shuffle(source)
 
     for there in along_x:
         pl.semaphore_signal(near_sem, inc=1, device_id=there, device_id_type=MESH)
-    loads[1].wait()
     loads[2].wait()
-    for k in range(4):
-        stacked = jnp.concatenate(
-            [
-                root[p, 16 * k : 16 * k + 16, 256 * q : 256 * q + 256]
-                for p in range(2)
-                for root in (lroot, rroot)
-                for q in range(4)
-            ],
-            axis=0,
-        )
-        roots_out[256 * k : 256 * k + 256, :] = mix(perm[ROOTS_OUT], stacked)
+    loads[3].wait()
+    for n, root in enumerate((rroot, lroot)):
+        for k in range(4):
+            stacked = jnp.concatenate(
+                [root[p, 16 * k : 16 * k + 16, 128 * q : 128 * q + 128] for p in range(2) for q in range(8)], axis=0
+            )
+            roots_out[n, 256 * k : 256 * k + 256, :] = mix(perm[ROOTS_OUT], stacked)
     pl.semaphore_wait(near_sem, len(along_x))
-    a1 = Plane(roots_out, roots_in, a1_sem, (z, o))
-    a1.start()
+    a1 = [Plane(roots_out.at[n], roots_in.at[n], a1_sem.at[n], (z, o)) for n in range(2)]
+    for exchange in a1:
+        exchange.start()
 
     rs_step(2)
 
-    loads[3].wait()
     loads[4].wait()
+    loads[5].wait()
     places = [owner_ref[b] * 2 + slot_ref[b] for b in range(BLOCKS)]
     row, column = iotas(16, WIDTH)
     for b in range(BLOCKS):
@@ -334,11 +339,18 @@
         to_places[256 * k : 256 * k + 256, :] = one_hot(row == target)
 
     rs_step(3)
+
+    for q in range(4):
+        row, column = iotas(WIDTH, 256)
+        chosen = ((column >> 2) & 15) * 64 + 16 * q + ((column >> 6) & 3) * 4 + (column & 3)
+        order[:, 256 * q : 256 * q + 256] = one_hot(row == chosen)
+
     rs_step(4)
     rs_step(5)
 
-    a1.wait(1)
-    blocks_out[...] = mix(to_blocks[...], roots_in[...])
+    for n in range(2):
+        a1[n].wait(1)
+        blocks_out[n] = mix(to_blocks[...], roots_in[n])
 
     rs_step(6)
     rs_step(7)
@@ -369,20 +381,24 @@
     spread.begin(0)
     swap_copy(2 * chip + 1 - c).wait_recv()
     spread.begin(1)
-    a2 = Column(blocks_out, blocks_in, a2_sem, (z, chip, c))
-    a2.start()
+    a2 = [Column(blocks_out.at[n], blocks_in.at[n], a2_sem.at[n], (z, chip, c)) for n in range(2)]
+    a2[0].start()
+    spread.early()
+    a2[1].start()
     spread.middle()
-
-    a2.wait(1)
-    for h in range(2):
-        turned = mix(perm[ROOTS_IN], blocks_in[256 * h : 256 * h + 256, :])
-        for q in range(4):
-            lsel[32 * h : 32 * h + 32, 256 * q : 256 * q + 256] = turned[32 * q : 32 * q + 32]
-            rheld[chunk(chip * 64 + 32 * h, 32), 256 * q : 256 * q + 256] = turned[128 + 32 * q : 160 + 32 * q]
+    spread.late()
+
+    def rows_of_root(n, held, start):
+        a2[n].wait(1)
+        for h in range(2):
+            turned = mix(perm[RESULTS_IN], blocks_in[n, 256 * h : 256 * h + 256, :])
+            for q in range(8):
+                held[chunk(start + 32 * h, 32), 128 * q : 128 * q + 128] = turned[32 * q : 32 * q + 32]
+
+    rows_of_root(0, rheld, chip * 64)
     rspread = Spread(rheld, rheld_send, rheld_recv, (z, x, y, c))
     rspread.begin(0)
     rspread.begin(1)
-
     spread.end()
 
     def send_rows(n, product):
@@ -393,7 +409,8 @@
                 [rows64[n, 32 * h : 32 * h + 32, 128 * q : 128 * q + 128] for q in range(8)], axis=0
             )
             zout[n, 256 * h : 256 * h + 256, :] = mix(perm[RESULTS_OUT], stacked)
-        exchange = Column(zout.at[n], zin.at[n], z_sem.at[n], (z, chip, c))
+        arrive = arrived_ref.at[pl.ds(2048, 512)] if n == 2 else zin.at[n]
+        exchange = Column(zout.at[n], arrive, z_sem.at[n], (z, chip, c))
         exchange.start()
         return exchange
 
@@ -409,46 +426,36 @@
     )
     zr = send_rows(1, lambda q: jnp.dot(columns, block[:, 256 * q : 256 * q + 256], preferred_element_type=F32))
 
+    rspread.early()
+    rows_of_root(1, lsel, 0)
     rspread.middle()
     scaled = jnp.concatenate([mix(lsel[...], block[:, 256 * q : 256 * q + 256]) for q in range(4)], axis=1)
+    scaled = jnp.concatenate([mix(scaled, order[:, 256 * q : 256 * q + 256]) for q in range(4)], axis=1)
+    rspread.late()
+
+    rspread.end()
+    zp = send_rows(2, lambda q: jnp.dot(scaled, rheld[:, 256 * q : 256 * q + 256], preferred_element_type=F32))
 
     def to_owners(n, exchange):
         exchange.wait(1)
         stats_out[n] = mix(to_places[...], zin[n])
-        owners = Plane(stats_out.at[n], stats_held.at[n], f_sem.at[n], (z, o))
+        owners = Plane(stats_out.at[n], arrived_ref.at[pl.ds(1024 * n, 1024)], f_sem.at[n], (z, o))
         owners.start()
         return owners
 
     fl = to_owners(0, zl)
-
-    rspread.end()
-    for n in range(4):
-        turned = mix(perm[RIGHT_ROWS], rheld[256 * n : 256 * n + 256, :])
-        for zz in range(PLANES):
-            rfull[64 * zz + 16 * n : 64 * zz + 16 * n + 16, :] = turned[16 * zz : 16 * zz + 16]
-    zp = send_rows(2, lambda q: jnp.dot(scaled, rfull[:, 256 * q : 256 * q + 256], preferred_element_type=F32))
-
     fr = to_owners(1, zr)
 
-    fl.wait(1)
-    stores = [pltpu.make_async_copy(stats_held.at[0], arrived_ref.at[pl.ds(0, 1024)], load_sem.at[0])]
-    stores[0].start()
-    fr.wait(1)
-    stores.append(pltpu.make_async_copy(stats_held.at[1], arrived_ref.at[pl.ds(1024, 1024)], load_sem.at[1]))
-    stores[1].start()
-    zp.wait(1)
-    stores.append(pltpu.make_async_copy(zin.at[2], arrived_ref.at[pl.ds(2048, 512)], load_sem.at[2]))
-    stores[2].start()
+    for exchange in (fl, fr, zp):
+        exchange.wait(1)
 
     ref = parts.at[pl.ds(0, 15)]
     pltpu.make_async_copy(ref, ref, rs_send).wait()
     swap_copy(o).wait_send()
     spread.sent()
     rspread.sent()
-    for exchange in (a1, a2, zl, zr, zp, fl, fr):
+    for exchange in (*a1, *a2, zl, zr, zp, fl, fr):
         exchange.wait(0)
-    for store in stores:
-        store.wait()
 
 
 def finish(arrived_ref, lstat_ref, rstat_ref, precond_ref, left_ref, right_ref):
@@ -476,7 +483,7 @@
         kernel,
         out_shape=jax.ShapeDtypeStruct((2560, 128), BF16),
         in_specs=[hbm] * 5,
-        out_specs=hbm,
+        out_specs=vmem,
         scratch_shapes=[
             pltpu.SMEM((BLOCKS,), jnp.int32),
             pltpu.SMEM((BLOCKS,), jnp.int32),
@@ -489,21 +496,20 @@
             pltpu.VMEM((8, 64, WIDTH), BF16),
             pltpu.VMEM((32, WIDTH), BF16),
             pltpu.VMEM((WIDTH, WIDTH), BF16),
-            pltpu.VMEM((1024, 256), BF16),
-            pltpu.VMEM((1024, 256), BF16),
-            pltpu.VMEM((512, 256), BF16),
-            pltpu.VMEM((512, 256), BF16),
+            pltpu.VMEM((2, 1024, 128), BF16),
+            pltpu.VMEM((2, 1024, 128), BF16),
+            pltpu.VMEM((2, 512, 128), BF16),
+            pltpu.VMEM((2, 512, 128), BF16),
             pltpu.VMEM((64, WIDTH), BF16),
             pltpu.VMEM((WIDTH, WIDTH), BF16),
             pltpu.VMEM((WIDTH, WIDTH), BF16),
             pltpu.VMEM((3, 64, WIDTH), BF16),
             pltpu.VMEM((3, 512, 128), BF16),
-            pltpu.VMEM((3, 512, 128), BF16),
-            pltpu.VMEM((2, 1024, 128), BF16),
+            pltpu.VMEM((2, 512, 128), BF16),
             pltpu.VMEM((2, 1024, 128), BF16),
             pltpu.VMEM((512, 1024), BF16),
             pltpu.VMEM((1024, 512), BF16),
-            dma((5,)),
+            dma((6,)),
             pltpu.SemaphoreType.REGULAR,
             dma,
             dma((8, SUBS)),
@@ -513,8 +519,8 @@
             dma((2, 4, 4, 2)),
             dma,
             dma((2, 4, 4, 2)),
-            dma((2,)),
-            dma((2,)),
+            dma((2, 2)),
+            dma((2, 2)),
             dma((3, 2)),
             dma((2, 2)),
         ],

time: 94.4 us -> 90.5 us (0.959)
  Pallas kernels: 92.4 us -> 88.5 us
    pallas_call x1, Pallas kernels: 91.1 us -> 87.2 us  [step(): pl.pallas_call(kernel, out_shape=jax.ShapeDtypeStruct((2560, 128), BF16),...]
where the time goes in v3:
time: 90.5 us; the launch traced here: 90.3 us
  Pallas kernels  88.5 us (98%)
  local copies, waits for them, and re-layouts  1.09 us (1%)
    pallas_call x1, Pallas kernels, step(): pl.pallas_call(kernel, out_shape=jax.ShapeDtypeStruct((2560, 128), BF16),...  87.2 us

profile of v3, /device:TPU:1, one launch (start us, length us, event | category | flops | bytes accessed | tf_op | source)
XLA Modules:
  0.0 90.3 jit_solution(10152621034952343203)
XLA Ops:
  0.6 0.0 copy-start.2
  0.6 0.0 copy-start.1
  0.7 87.2 %shard_map.94.arrived_ref = bf16[2560,128]{1,0:T(8,128)(2,1)} custom-call(s32[32]{0:T(128)} %owner_hbm.1, s32[32]{0:T(128)} %slot_hbm.1, bf16[1,32,32768]{2,1,0:T(8,128)(2,1)} %g_hbm.1, bf16[2,64,1024]{2,1,0:T(8,128)(2,1)} %lroot_hbm.1, bf16[2,64,1024]{2,1,0:T(8,128)(2,1)} %rroot_hbm.1), custom_call_target="tpu_custom_call" | custom-call | tf_op jit(solution)/shard_map/pallas_call | solution.py:482
  87.8 0.0 copy-done.2
  87.9 0.0 copy-done.1
  87.9 0.0 copy-start
  87.9 1.1 %copy-done = bf16[2560,128]{1,0:T(8,128)(2,1)S(1)} copy-done((bf16[2560,128]{1,0:T(8,128)(2,1)S(1)}, bf16[2560,128]{1,0:T(8,128)(2,1)}, u32[]{:S(2)}) %copy-start) | copy-done | bytes 655384
  89.0 1.3 %shard_map.95 = (bf16[32,2048]{1,0:T(8,128)(2,1)}, f32[2,64,1024]{2,1,0:T(8,128)}, f32[2,64,1024]{2,1,0:T(8,128)}) custom-call(bf16[2560,128]{1,0:T(8,128)(2,1)S(1)} %copy-done, f32[2,64,1024]{2,1,0:T(8,128)S(1)} %copy-done.1, f32[2,64,1024]{2,1,0:T(8,128)S(1)} %copy-done.2), custom_call_target="tpu_custom_call" | custom-call | tf_op jit(solution)/shard_map/pallas_call | solution.py:531
Async XLA Ops:
  0.6 87.2 %copy-start.2 = (f32[2,64,1024]{2,1,0:T(8,128)S(1)}, f32[2,64,1024]{2,1,0:T(8,128)}, u32[]{:S(2)}) copy-start(f32[2,64,1024]{2,1,0:T(8,128)} %rstat_ref.1) | copy-start | bytes 1572868
  0.6 87.2 %copy-start.1 = (f32[2,64,1024]{2,1,0:T(8,128)S(1)}, f32[2,64,1024]{2,1,0:T(8,128)}, u32[]{:S(2)}) copy-start(f32[2,64,1024]{2,1,0:T(8,128)} %lstat_ref.1) | copy-start | bytes 1572868
  87.9 1.1 %copy-start = (bf16[2560,128]{1,0:T(8,128)(2,1)S(1)}, bf16[2560,128]{1,0:T(8,128)(2,1)}, u32[]{:S(2)}) copy-start(bf16[2560,128]{1,0:T(8,128)(2,1)} %shard_map.94.arrived_ref) | copy-start | bytes 1966084

commit v4 on v3

--- a/solution.py
+++ b/solution.py
@@ -46,7 +46,7 @@
     return (m % 16) * 16 + m // 16
 
 
-def roots_out(m):
+def roots_out_rows(m):
     return (((m >> 4) & 1) * 8 + (m & 7)) * 16 + (m >> 5) * 2 + ((m >> 3) & 1)
 
 
@@ -67,7 +67,6 @@
     return one_hot(k == source(m))
 
 
-SHUFFLES = (transpose16, roots_out, results_in, results_out)
 T16, ROOTS_OUT, RESULTS_IN, RESULTS_OUT = range(4)
 
 
@@ -246,7 +245,7 @@
     loads = [
         pltpu.make_async_copy(src, dst, load_sem.at[n])
         for n, (src, dst) in enumerate(
-            ((g_hbm.at[0, halves[0]], g.at[halves[0]]), (g_hbm.at[0, halves[1]], g.at[halves[1]]), (lroot_hbm, lroot), (rroot_hbm, rroot), (owner_hbm, owner_ref), (slot_hbm, slot_ref))
+            ((g_hbm.at[0, halves[0]], g.at[halves[0]]), (g_hbm.at[0, halves[1]], g.at[halves[1]]), (rroot_hbm, rroot), (lroot_hbm, lroot), (owner_hbm, owner_ref), (slot_hbm, slot_ref))
         )
     ]
     for load in loads:
@@ -303,25 +302,26 @@
     loads[1].wait()
     make_parts(1 - first_half)
     rs_step(1)
-    for n, source in enumerate(SHUFFLES[1:]):
-        perm[n + 1] = shuffle(source)
 
     for there in along_x:
         pl.semaphore_signal(near_sem, inc=1, device_id=there, device_id_type=MESH)
-    loads[2].wait()
-    loads[3].wait()
-    for n, root in enumerate((rroot, lroot)):
+    a1 = [Plane(roots_out.at[n], roots_in.at[n], a1_sem.at[n], (z, o)) for n in range(2)]
+
+    def send_roots(n, root):
+        loads[2 + n].wait()
         for k in range(4):
             stacked = jnp.concatenate(
                 [root[p, 16 * k : 16 * k + 16, 128 * q : 128 * q + 128] for p in range(2) for q in range(8)], axis=0
             )
             roots_out[n, 256 * k : 256 * k + 256, :] = mix(perm[ROOTS_OUT], stacked)
+        a1[n].start()
+
+    perm[ROOTS_OUT] = shuffle(roots_out_rows)
     pl.semaphore_wait(near_sem, len(along_x))
-    a1 = [Plane(roots_out.at[n], roots_in.at[n], a1_sem.at[n], (z, o)) for n in range(2)]
-    for exchange in a1:
-        exchange.start()
-
+    send_roots(0, rroot)
     rs_step(2)
+    send_roots(1, lroot)
+    rs_step(3)
 
     loads[4].wait()
     loads[5].wait()
@@ -329,6 +329,29 @@
     row, column = iotas(16, WIDTH)
     for b in range(BLOCKS):
         to_blocks[16 * b : 16 * b + 16, :] = one_hot(column == places[b] * 16 + row)
+    rs_step(4)
+
+    def make_order(q):
+        row, column = iotas(WIDTH, 256)
+        chosen = ((column >> 2) & 15) * 64 + 16 * q + ((column >> 6) & 3) * 4 + (column & 3)
+        order[:, 256 * q : 256 * q + 256] = one_hot(row == chosen)
+
+    perm[RESULTS_IN] = shuffle(results_in)
+    make_order(0)
+    make_order(1)
+    rs_step(5)
+
+    a1[0].wait(1)
+    blocks_out[0] = mix(to_blocks[...], roots_in[0])
+    perm[RESULTS_OUT] = shuffle(results_out)
+    make_order(2)
+    rs_step(6)
+
+    a1[1].wait(1)
+    blocks_out[1] = mix(to_blocks[...], roots_in[1])
+    make_order(3)
+    rs_step(7)
+
     column = lax.broadcasted_iota(jnp.int32, (1, 512), 1)
     target = jnp.zeros((1, 512), jnp.int32)
     for b in range(BLOCKS):
@@ -337,23 +360,6 @@
     for k in range(4):
         row = lax.broadcasted_iota(jnp.int32, (256, 512), 0) + 256 * k
         to_places[256 * k : 256 * k + 256, :] = one_hot(row == target)
-
-    rs_step(3)
-
-    for q in range(4):
-        row, column = iotas(WIDTH, 256)
-        chosen = ((column >> 2) & 15) * 64 + 16 * q + ((column >> 6) & 3) * 4 + (column & 3)
-        order[:, 256 * q : 256 * q + 256] = one_hot(row == chosen)
-
-    rs_step(4)
-    rs_step(5)
-
-    for n in range(2):
-        a1[n].wait(1)
-        blocks_out[n] = mix(to_blocks[...], roots_in[n])
-
-    rs_step(6)
-    rs_step(7)
 
     def last_sum(which):
         rows = chunk(which * 32, 32)
@@ -427,12 +433,11 @@
     zr = send_rows(1, lambda q: jnp.dot(columns, block[:, 256 * q : 256 * q + 256], preferred_element_type=F32))
 
     rspread.early()
+    rspread.middle()
+    rspread.late()
     rows_of_root(1, lsel, 0)
-    rspread.middle()
     scaled = jnp.concatenate([mix(lsel[...], block[:, 256 * q : 256 * q + 256]) for q in range(4)], axis=1)
     scaled = jnp.concatenate([mix(scaled, order[:, 256 * q : 256 * q + 256]) for q in range(4)], axis=1)
-    rspread.late()
-
     rspread.end()
     zp = send_rows(2, lambda q: jnp.dot(scaled, rheld[:, 256 * q : 256 * q + 256], preferred_element_type=F32))
 
@@ -490,7 +495,7 @@
             pltpu.VMEM((32, 32 * WIDTH), BF16),
             pltpu.VMEM((2, 64, WIDTH), BF16),
             pltpu.VMEM((2, 64, WIDTH), BF16),
-            pltpu.VMEM((len(SHUFFLES), 256, 256), BF16),
+            pltpu.VMEM((4, 256, 256), BF16),
             pltpu.VMEM((16, 64, WIDTH), BF16),
             pltpu.VMEM((8, 64, WIDTH), BF16),
             pltpu.VMEM((8, 64, WIDTH), BF16),

time: 90.5 us -> 89.5 us (0.989)
  Pallas kernels: 88.5 us -> 87.5 us
    pallas_call x1, Pallas kernels: 87.2 us -> 86.2 us  [step(): pl.pallas_call(kernel, out_shape=jax.ShapeDtypeStruct((2560, 128), BF16),...]
where the time goes in v4:
time: 89.5 us; the launch traced here: 89.3 us
  Pallas kernels  87.5 us (98%)
  local copies, waits for them, and re-layouts  1.09 us (1%)
    pallas_call x1, Pallas kernels, step(): pl.pallas_call(kernel, out_shape=jax.ShapeDtypeStruct((2560, 128), BF16),...  86.2 us

profile of v4, /device:TPU:1, one launch (start us, length us, event | category | flops | bytes accessed | tf_op | source)
XLA Modules:
  0.0 89.3 jit_solution(2049376127083990352)
XLA Ops:
  0.6 0.0 copy-start.2
  0.6 0.0 copy-start.1
  0.7 86.2 %shard_map.94.arrived_ref = bf16[2560,128]{1,0:T(8,128)(2,1)} custom-call(s32[32]{0:T(128)} %owner_hbm.1, s32[32]{0:T(128)} %slot_hbm.1, bf16[1,32,32768]{2,1,0:T(8,128)(2,1)} %g_hbm.1, bf16[2,64,1024]{2,1,0:T(8,128)(2,1)} %lroot_hbm.1, bf16[2,64,1024]{2,1,0:T(8,128)(2,1)} %rroot_hbm.1), custom_call_target="tpu_custom_call" | custom-call | tf_op jit(solution)/shard_map/pallas_call | solution.py:487
  86.9 0.0 copy-done.2
  86.9 0.0 copy-done.1
  86.9 0.0 copy-start
  86.9 1.1 %copy-done = bf16[2560,128]{1,0:T(8,128)(2,1)S(1)} copy-done((bf16[2560,128]{1,0:T(8,128)(2,1)S(1)}, bf16[2560,128]{1,0:T(8,128)(2,1)}, u32[]{:S(2)}) %copy-start) | copy-done | bytes 655384
  88.0 1.3 %shard_map.95 = (bf16[32,2048]{1,0:T(8,128)(2,1)}, f32[2,64,1024]{2,1,0:T(8,128)}, f32[2,64,1024]{2,1,0:T(8,128)}) custom-call(bf16[2560,128]{1,0:T(8,128)(2,1)S(1)} %copy-done, f32[2,64,1024]{2,1,0:T(8,128)S(1)} %copy-done.1, f32[2,64,1024]{2,1,0:T(8,128)S(1)} %copy-done.2), custom_call_target="tpu_custom_call" | custom-call | tf_op jit(solution)/shard_map/pallas_call | solution.py:536
Async XLA Ops:
  0.6 86.3 %copy-start.2 = (f32[2,64,1024]{2,1,0:T(8,128)S(1)}, f32[2,64,1024]{2,1,0:T(8,128)}, u32[]{:S(2)}) copy-start(f32[2,64,1024]{2,1,0:T(8,128)} %rstat_ref.1) | copy-start | bytes 1572868
  0.6 86.3 %copy-start.1 = (f32[2,64,1024]{2,1,0:T(8,128)S(1)}, f32[2,64,1024]{2,1,0:T(8,128)}, u32[]{:S(2)}) copy-start(f32[2,64,1024]{2,1,0:T(8,128)} %lstat_ref.1) | copy-start | bytes 1572868
  86.9 1.1 %copy-start = (bf16[2560,128]{1,0:T(8,128)(2,1)S(1)}, bf16[2560,128]{1,0:T(8,128)(2,1)}, u32[]{:S(2)}) copy-start(bf16[2560,128]{1,0:T(8,128)(2,1)} %shard_map.94.arrived_ref) | copy-start | bytes 1966084
